TPU v7x, 1024 devices: a whole 4x4x32 slice. The times are simulated.
1024 devices in a mesh: dp: 64 (over z_lo, x, core), seq: 16 (over z_hi, y).
Axes of the slice: x: 4, y: 4, z: 32 (z_hi: 4, z_lo: 8; z = z_hi * 8 + z_lo), core: 2. Of those that a mesh axis runs over, the one named last changes fastest.
Arguments:
- queries: bfloat16 [131072, 4096], P(('dp', 'seq')), may hold values from -300 to 300
- key_proj: bfloat16 [131072, 512], P(('dp', 'seq')), may hold values from -4.5 to 4.5
- value_proj: bfloat16 [131072, 512], P(('dp', 'seq')), may hold values from -6 to 6
- seq_lengths: int32 [256], replicated, may hold values from 1 to 1025, 131072 in all
Outputs:
- attended: bfloat16 [131072, 4096], P(('dp', 'seq'))
Inputs may be any that keep to these rules, and one draw needn't show every extreme that they name: `seq_lengths`: the sequences cover all 131072 tokens; the longest has exactly 1025 tokens.
All inputs are finite; a program needn't handle non-finite values.
Results may differ from a plain program's by a relative error of at most 0.0036.
Values may be sent and summed in bfloat16 or wider, within the bound.
A program may use at most 32 MiB of HBM per device.

v0:
```python
import math

import jax
import jax.numpy as jnp
from jax import lax
from jax.sharding import PartitionSpec as P

HD = 128
QH = 32
KVH = 4


score_scale = 0.08838834764831845
neg_fill = -1e30


def from_behind(block, axis, distance):
    devices = range(lax.axis_size(axis))
    route = [(i - distance, i) for i in devices if i - distance in devices]
    return lax.ppermute(block, axis, route)


def segment_starts(seq_lengths, positions):
    seq_ends = jnp.cumsum(seq_lengths)
    begins = seq_ends - seq_lengths
    covered = begins[None, :] <= positions[:, None]
    return jnp.max(jnp.where(covered, begins[None, :], 0), axis=1)


def attend(
    queries,
    own_keys,
    own_values,
    tail_keys,
    tail_values,
    query_pos,
    key_pos,
    tail_pos,
    query_start,
    tail_limit,
):
    row_count = queries.shape[0]
    heads_query = queries.shape[1]
    group_size = heads_query // own_keys.shape[1]
    tile_rows = math.gcd(row_count, 512)
    pieces = []
    for offset in range(0, row_count, tile_rows):
        query_tile = queries[offset : offset + tile_rows]
        pos_tile = query_pos[offset : offset + tile_rows]
        start_tile = query_start[offset : offset + tile_rows]
        key_count = offset + tile_rows
        keys_used = own_keys[:key_count]
        values_used = own_values[:key_count]
        pos_used = key_pos[:key_count]
        own_mask = (pos_used[None, :] <= pos_tile[:, None]) & (
            pos_used[None, :] >= start_tile[:, None]
        )
        use_tail = offset < tail_limit
        tail_mask = tail_pos[None, :] >= start_tile[:, None]

        def one_head(head_index):
            shared_index = head_index // group_size
            query_head = lax.dynamic_index_in_dim(query_tile, head_index, 1, keepdims=False)
            key_head = lax.dynamic_index_in_dim(keys_used, shared_index, 1, keepdims=False)
            value_head = lax.dynamic_index_in_dim(values_used, shared_index, 1, keepdims=False)
            own_scores = (
                jnp.einsum("qd,kd->qk", query_head, key_head, preferred_element_type=jnp.float32)
                * score_scale
            )
            own_scores = jnp.where(own_mask, own_scores, neg_fill)
            row_max = jnp.max(own_scores, axis=1)
            if use_tail:
                tail_key = lax.dynamic_index_in_dim(tail_keys, shared_index, 1, keepdims=False)
                tail_value = lax.dynamic_index_in_dim(tail_values, shared_index, 1, keepdims=False)
                raw = (
                    jnp.einsum(
                        "qd,kd->qk", query_head, tail_key, preferred_element_type=jnp.float32
                    )
                    * score_scale
                )
                tail_scores = jnp.where(tail_mask, raw, neg_fill)
                row_max = jnp.maximum(row_max, jnp.max(tail_scores, axis=1))
            own_weights = jnp.where(own_mask, jnp.exp(own_scores - row_max[:, None]), 0.0)
            row_sum = jnp.sum(own_weights, axis=1)
            weighted = jnp.dot(
                own_weights.astype(jnp.bfloat16), value_head, preferred_element_type=jnp.float32
            )
            if use_tail:
                tail_weights = jnp.where(tail_mask, jnp.exp(tail_scores - row_max[:, None]), 0.0)
                row_sum = row_sum + jnp.sum(tail_weights, axis=1)
                weighted = weighted + jnp.dot(
                    tail_weights.astype(jnp.bfloat16),
                    tail_value,
                    preferred_element_type=jnp.float32,
                )
            return (weighted / row_sum[:, None]).astype(jnp.bfloat16)

        per_head = lax.map(one_head, jnp.arange(heads_query, dtype=jnp.int32))
        pieces.append(jnp.transpose(per_head, (1, 0, 2)))
    return jnp.concatenate(pieces, axis=0)


def body(queries, key_proj, value_proj, seq_lengths):
    tok_rows = queries.shape[0]
    members = lax.axis_size("seq")
    home_index = lax.axis_index("dp")
    block_rows = tok_rows * members
    reach_rows = block_rows // 2
    block_start = home_index * block_rows
    key_pos = block_start + jnp.arange(block_rows, dtype=jnp.int32)
    tail_pos = block_start - reach_rows + jnp.arange(reach_rows, dtype=jnp.int32)
    local_heads = QH // members
    copies = max(1, members // KVH)
    query_split = queries.reshape(tok_rows, members, local_heads * HD)
    key_split = key_proj.reshape(tok_rows, KVH, HD)
    value_split = value_proj.reshape(tok_rows, KVH, HD)
    key_split = jnp.repeat(key_split, copies, axis=1)
    value_split = jnp.repeat(value_split, copies, axis=1)
    query_block, key_block, value_block = (
        lax.all_to_all(query_split, "seq", split_axis=1, concat_axis=0, tiled=True),
        lax.all_to_all(key_split, "seq", split_axis=1, concat_axis=0, tiled=True),
        lax.all_to_all(value_split, "seq", split_axis=1, concat_axis=0, tiled=True),
    )
    query_block = query_block.reshape(block_rows, local_heads, HD)
    tail_keys, tail_values = from_behind(
        (key_block[reach_rows:], value_block[reach_rows:]), "dp", 1
    )
    starts = segment_starts(seq_lengths, key_pos)
    mixed = attend(
        query_block,
        key_block,
        value_block,
        tail_keys,
        tail_values,
        key_pos,
        key_pos,
        tail_pos,
        starts,
        reach_rows,
    )
    mixed = mixed.reshape(block_rows, 1, local_heads * HD)
    returned = lax.all_to_all(mixed, "seq", split_axis=0, concat_axis=1, tiled=True)
    return returned.reshape(tok_rows, QH * HD)


def solution(mesh):
    return jax.shard_map(
        body,
        mesh=mesh,
        in_specs=(P(("dp", "seq"), None), P(("dp", "seq"), None), P(("dp", "seq"), None), P()),
        out_specs=P(("dp", "seq"), None),
        check_vma=False,
    )
```

profile of v0, /device:TPU:70, one launch (start us, length us, event | category | flops | bytes accessed | tf_op | source)
XLA Modules:
  0.0 409.2 jit_solution(6369359316067699744)
XLA Ops:
  1.8 29.3 %all-to-all-start.1 = ((bf16[128,16,128]{2,0,1:T(8,128)(2,1)}), bf16[128,16,128]{2,0,1:T(8,128)(2,1)S(1)}, u32[]{:S(2)}, u32[]{:S(2)}) async-start(bf16[128,16,128]{2,0,1:T(8,128)(2,1)} %bitcast.2), calls=%async_computation.1 | async-start | bytes 1048576 | tf_op jit(solution)/shard_map/all_to_all | solution.py:121
  32.0 51.8 %all-to-all-done.1 = bf16[128,16,128]{2,0,1:T(8,128)(2,1)S(1)} async-done(((bf16[128,16,128]{2,0,1:T(8,128)(2,1)}), bf16[128,16,128]{2,0,1:T(8,128)(2,1)S(1)}, u32[]{:S(2)}, u32[]{:S(2)}) %all-to-all-start.1) | async-done | bytes 524320 | tf_op jit(solution)/shard_map/all_to_all | solution.py:121
  84.8 8.2 %all-to-all-start.2 = ((bf16[128,16,128]{2,0,1:T(8,128)(2,1)}), bf16[128,16,128]{2,0,1:T(8,128)(2,1)S(1)}, u32[]{:S(2)}, u32[]{:S(2)}) async-start(bf16[128,16,128]{2,0,1:T(8,128)(2,1)} %bitcast.8), calls=%async_computation.2 | async-start | bytes 1048576 | tf_op jit(solution)/shard_map/all_to_all | solution.py:122
  94.1 34.1 %all-to-all-done.2 = bf16[128,16,128]{2,0,1:T(8,128)(2,1)S(1)} async-done(((bf16[128,16,128]{2,0,1:T(8,128)(2,1)}), bf16[128,16,128]{2,0,1:T(8,128)(2,1)S(1)}, u32[]{:S(2)}, u32[]{:S(2)}) %all-to-all-start.2) | async-done | bytes 524320 | tf_op jit(solution)/shard_map/all_to_all | solution.py:122
  128.2 32.9 %all-to-all-start = ((bf16[128,16,256]{2,0,1:T(8,128)(2,1)}), bf16[128,16,256]{2,0,1:T(8,128)(2,1)S(1)}, u32[]{:S(2)}, u32[]{:S(2)}) async-start(bf16[128,16,256]{2,0,1:T(8,128)(2,1)} %bitcast.148), calls=%async_computation | async-start | bytes 2097152 | tf_op jit(solution)/shard_map/all_to_all | solution.py:120
  167.4 1.9 collective-permute-start
  170.1 14.5 %collective-permute-start.1 = (bf16[1024,1,128]{2,0,1:T(8,128)(2,1)}, bf16[1024,1,128]{2,0,1:T(8,128)(2,1)}, u32[]{:S(2)}, u32[]{:S(2)}) collective-permute-start(bf16[1024,1,128]{2,0,1:T(8,128)(2,1)} %bitcast.13), channel_id=1, source_target_pairs={{0,16},{16,32},{32,48},{48,64},{64,80},{80,96},{96,112},{112,128},... | collective-permute-start | bytes 786440 | tf_op jit(solution)/shard_map/ppermute | solution.py:20
  184.7 66.9 %all-to-all-done = bf16[128,16,256]{2,0,1:T(8,128)(2,1)S(1)} async-done(((bf16[128,16,256]{2,0,1:T(8,128)(2,1)}), bf16[128,16,256]{2,0,1:T(8,128)(2,1)S(1)}, u32[]{:S(2)}, u32[]{:S(2)}) %all-to-all-start) | async-done | bytes 1048608 | tf_op jit(solution)/shard_map/all_to_all | solution.py:120
  251.9 16.4 %while.47 = (s32[]{:T(128)}, bf16[2,512,128]{1,2,0:T(8,128)(2,1)S(1)}, s32[2]{0:T(128)S(1)}, bf16[512,2,128]{2,0,1:T(8,128)(2,1)S(1)}, bf16[2048,1,128]{2,0,1:T(...) while((s32[]{:T(128)}, ...), condition=%wide.region_22.23_spmd.clone, body=%wide.region_19.22_spmd.clone.sunk | while | flops 560069632 | bytes 14481643 | solution.py:98
  254.4 2.0 fusion.164
  256.4 1.7 fusion.165
  258.1 1.8 fusion.166
  262.6 2.0 fusion.164
  264.6 1.7 fusion.165
  266.3 1.8 fusion.166
  268.5 14.0 %while.46 = (s32[]{:T(128)}, bf16[2,512,128]{1,2,0:T(8,128)(2,1)S(1)}, s32[2]{0:T(128)S(1)}, bf16[512,2,128]{2,0,1:T(8,128)(2,1)S(1)}, bf16[1536,1,128]{2,0,1:T(...) while((s32[]{:T(128)}, ...), condition=%wide.region_18.19_spmd.clone, body=%wide.region_15.18_spmd.clone.sunk | while | flops 416939008 | bytes 12626127 | solution.py:98
  271.0 2.0 fusion.159
  278.0 2.0 fusion.159
  282.7 18.2 %while.49 = (s32[]{:T(128)}, bf16[2,512,128]{1,2,0:T(8,128)(2,1)S(1)}, s32[2]{0:T(128)S(1)}, bf16[512,2,128]{2,0,1:T(8,128)(2,1)S(1)}, bf16[1024,1,128]{2,0,1:T(...) while((s32[]{:T(128)}, ...), condition=%wide.region_14.15_spmd.clone.clone, body=%wide.region_9.14_spmd.clone.clone.sunk | while | flops 556989440 | bytes 17238224 | solution.py:98
  285.7 2.0 fusion.184
  290.1 1.6 fusion.187
  294.8 2.0 fusion.184
  301.1 15.7 %while.48 = (s32[]{:T(128)}, bf16[2,512,128]{1,2,0:T(8,128)(2,1)S(1)}, s32[2]{0:T(128)S(1)}, bf16[512,2,128]{2,0,1:T(8,128)(2,1)S(1)}, bf16[512,1,128]{2,0,1:T(8...) while((s32[]{:T(128)}, ...), condition=%wide.region_8.9_spmd.clone.clone, body=%wide.region_3.8_spmd.clone.clone.sunk | while | flops 415955968 | bytes 11729095 | solution.py:98
  319.7 86.2 %all_to_all.66 = bf16[16,2,16384]{2,1,0:T(2,128)(2,1)S(1)} all-to-all(bf16[16,2,16384]{2,1,0:T(2,128)(2,1)S(1)} %reshape.108), channel_id=1, replica_groups=mesh['dp'=64,'seq'=16] {'seq'}, dimensions={0} | all-to-all | bytes 2097152 | tf_op jit(solution)/shard_map/all_to_all | solution.py:142
  (140 shorter events, 46.2 us)
Async XLA Ops:
  0.0 0.9 copy-start
  0.0 93.0 %copy-start.1 = (bf16[128,4096]{1,0:T(8,128)(2,1)S(1)}, bf16[128,4096]{1,0:T(8,128)(2,1)}, u32[]{:S(2)}) copy-start(bf16[128,4096]{1,0:T(8,128)(2,1)} %param.12) | copy-start | bytes 3145732
  1.8 82.1 %all-to-all-start.1 = ((bf16[128,16,128]{2,0,1:T(8,128)(2,1)}), bf16[128,16,128]{2,0,1:T(8,128)(2,1)S(1)}, u32[]{:S(2)}, u32[]{:S(2)}) async-start(bf16[128,16,128]{2,0,1:T(8,128)(2,1)} %bitcast.2), calls=%async_computation.1 | async-start | bytes 1048576 | tf_op jit(solution)/shard_map/all_to_all | solution.py:121
  84.8 43.5 %all-to-all-start.2 = ((bf16[128,16,128]{2,0,1:T(8,128)(2,1)}), bf16[128,16,128]{2,0,1:T(8,128)(2,1)S(1)}, u32[]{:S(2)}, u32[]{:S(2)}) async-start(bf16[128,16,128]{2,0,1:T(8,128)(2,1)} %bitcast.8), calls=%async_computation.2 | async-start | bytes 1048576 | tf_op jit(solution)/shard_map/all_to_all | solution.py:122
  93.0 68.1 %copy-start.14 = (s32[256]{0:T(256)S(1)}, s32[256]{0:T(256)}, u32[]{:S(2)}) copy-start(s32[256]{0:T(256)} %param.15) | copy-start | bytes 3076
  128.2 123.4 %all-to-all-start = ((bf16[128,16,256]{2,0,1:T(8,128)(2,1)}), bf16[128,16,256]{2,0,1:T(8,128)(2,1)S(1)}, u32[]{:S(2)}, u32[]{:S(2)}) async-start(bf16[128,16,256]{2,0,1:T(8,128)(2,1)} %bitcast.148), calls=%async_computation | async-start | bytes 2097152 | tf_op jit(solution)/shard_map/all_to_all | solution.py:120
  167.4 115.3 %collective-permute-start = (bf16[1024,1,128]{2,0,1:T(8,128)(2,1)}, bf16[1024,1,128]{2,0,1:T(8,128)(2,1)}, u32[]{:S(2)}, u32[]{:S(2)}) collective-permute-start(bf16[1024,1,128]{2,0,1:T(8,128)(2,1)} %bitcast.7), channel_id=1, source_target_pairs={{0,16},{16,32},{32,48},{48,64},{64,80},{80,96},{96,112},{112,128},... | collective-permute-start | bytes 786440 | tf_op jit(solution)/shard_map/ppermute | solution.py:20
  170.1 112.5 %collective-permute-start.1 = (bf16[1024,1,128]{2,0,1:T(8,128)(2,1)}, bf16[1024,1,128]{2,0,1:T(8,128)(2,1)}, u32[]{:S(2)}, u32[]{:S(2)}) collective-permute-start(bf16[1024,1,128]{2,0,1:T(8,128)(2,1)} %bitcast.13), channel_id=1, source_target_pairs={{0,16},{16,32},{32,48},{48,64},{64,80},{80,96},{96,112},{112,128},... | collective-permute-start | bytes 786440 | tf_op jit(solution)/shard_map/ppermute | solution.py:20
  251.8 16.6 %copy-start.10 = (s32[512]{0:T(512)S(1)}, s32[512]{0:T(512)}, u32[]{:S(2)}) copy-start(s32[512]{0:T(512)} %get-tuple-element.911) | copy-start | bytes 6148
  251.8 16.6 %copy-start.11 = (s32[512]{0:T(512)S(1)}, s32[512]{0:T(512)}, u32[]{:S(2)}) copy-start(s32[512]{0:T(512)} %get-tuple-element.910) | copy-start | bytes 6148
  254.4 2.0 copy-start.12
  254.4 2.0 copy-start.13
  262.6 2.0 copy-start.12
  262.6 2.0 copy-start.13
  268.5 14.2 %copy-start.3 = (bf16[8,128,1,128]{3,1,0,2:T(8,128)(2,1)S(1)}, bf16[8,128,1,128]{3,1,0,2:T(8,128)(2,1)}, u32[]{:S(2)}) copy-start(bf16[8,128,1,128]{3,1,0,2:T(8,128)(2,1)} %get-tuple-element.577) | copy-start | bytes 786436
  268.5 14.2 %copy-start.5 = (s32[1024]{0:T(1024)S(1)}, s32[1024]{0:T(1024)}, u32[]{:S(2)}) copy-start(s32[1024]{0:T(1024)} %slice.158) | copy-start | bytes 12292
  268.5 14.2 %copy-start.8 = (s32[512]{0:T(512)S(1)}, s32[512]{0:T(512)}, u32[]{:S(2)}) copy-start(s32[512]{0:T(512)} %get-tuple-element.949) | copy-start | bytes 6148
  268.5 14.2 %copy-start.9 = (s32[512]{0:T(512)S(1)}, s32[512]{0:T(512)}, u32[]{:S(2)}) copy-start(s32[512]{0:T(512)} %get-tuple-element.948) | copy-start | bytes 6148
  273.0 1.0 copy-start.2
  280.0 1.0 copy-start.2
  282.7 18.4 %copy-start.4 = (s32[512]{0:T(512)S(1)}, s32[512]{0:T(512)}, u32[]{:S(2)}) copy-start(s32[512]{0:T(512)} %get-tuple-element.993) | copy-start | bytes 6148
  282.7 18.4 %copy-start.6 = (bf16[4,128,1,128]{3,1,0,2:T(8,128)(2,1)S(1)}, bf16[4,128,1,128]{3,1,0,2:T(8,128)(2,1)}, u32[]{:S(2)}) copy-start(bf16[4,128,1,128]{3,1,0,2:T(8,128)(2,1)} %slice.147) | copy-start | bytes 393220
  282.7 18.4 %copy-start.7 = (bf16[4,128,1,128]{3,1,0,2:T(8,128)(2,1)S(1)}, bf16[4,128,1,128]{3,1,0,2:T(8,128)(2,1)}, u32[]{:S(2)}) copy-start(bf16[4,128,1,128]{3,1,0,2:T(8,128)(2,1)} %slice.149) | copy-start | bytes 393220
where the time goes:
time: 410 us; the launch traced here: 409 us
  waiting for transfers between devices  153 us (37%)
  starting transfers between devices  86.8 us (21%)
  blocking collectives  86.2 us (21%)
  matrix products  31.7 us (8%)
  local copies, waits for them, and re-layouts  21.5 us (5%)
  loops' own time  16.2 us (4%)
  other arithmetic  13.3 us (3%)
    all_to_all x1, blocking collectives, body(): lax.all_to_all(mixed, 'seq', split_axis=0, concat_axis=1, tiled=True)  86.2 us
    all_to_all x1, waiting for transfers between devices, body(): lax.all_to_all(query_split, 'seq', split_axis=1, concat_axis=0, tiled=True)  66.9 us
    all_to_all x1, waiting for transfers between devices, body(): lax.all_to_all(key_split, 'seq', split_axis=1, concat_axis=0, tiled=True)  51.8 us
    all_to_all x1, waiting for transfers between devices, body(): lax.all_to_all(value_split, 'seq', split_axis=1, concat_axis=0, tiled=True)  34.1 us
    all_to_all x1, starting transfers between devices, body(): lax.all_to_all(query_split, 'seq', split_axis=1, concat_axis=0, tiled=True)  32.9 us
    all_to_all x1, starting transfers between devices, body(): lax.all_to_all(key_split, 'seq', split_axis=1, concat_axis=0, tiled=True)  29.3 us
    ppermute x2, starting transfers between devices, from_behind(): return lax.ppermute(block, axis, route)  16.4 us
    another operation x4, loops' own time, attend(): per_head = lax.map(one_head, jnp.arange(heads_query, dtype=jnp.int32))  16.2 us
  transfers between devices with their start and end apart: 5, of which 3 were waited for; matrix products, arithmetic and copies ran while one was open for 8% of the time, Pallas kernels for 0%

commit v1 on v0

v1 whole, which is shorter than its diff:
```python
import functools

import jax
import jax.numpy as jnp
from jax import lax
from jax.experimental import pallas as pl
from jax.experimental.pallas import tpu as pltpu
from jax.sharding import PartitionSpec as P

HD = 128
QH = 32
KVH = 4
GROUP = QH // KVH
ROWS = 128
SLOTS = 9
AHEAD = 80
SCALE = 0.08838834764831845 * 1.4426950408889634
MASKED = -1e30
MESH = pl.DeviceIdType.MESH


def kernel(
    seq_size,
    total,
    len_ref,
    q_ref,
    k_ref,
    v_ref,
    o_ref,
    q_own,
    window,
    transit,
    scores,
    weights,
    peaks,
    inverse,
    bias,
    local_sem,
    z_send,
    y_send,
    arrived,
    passing,
):
    dp = lax.axis_index("dp")
    seq = lax.axis_index("seq")
    chunk = dp * seq_size + seq
    lane_y = seq % 4

    def at_chunk(offset):
        other = (chunk + offset + total) % total
        return (other // seq_size, other % seq_size)

    def at_y(turn):
        return (dp, seq - lane_y + (lane_y + turn) % 4)

    own = [
        pltpu.make_async_copy(q_ref, q_own, local_sem.at[0]),
        pltpu.make_async_copy(k_ref, window.at[0, 0], local_sem.at[1]),
        pltpu.make_async_copy(v_ref, window.at[1, 0], local_sem.at[2]),
    ]
    for copy in own:
        copy.start()

    barrier = pltpu.get_barrier_semaphore()
    for device in (at_chunk(-4), at_chunk(4), at_chunk(-12), at_y(1), at_y(2), at_y(3)):
        pl.semaphore_signal(barrier, inc=1, device_id=device, device_id_type=MESH)
    pl.semaphore_wait(barrier, 6)

    parts = (pl.ds(0, AHEAD), pl.ds(AHEAD, ROWS - AHEAD))
    mine = (k_ref, v_ref)

    def z_copy(kv, step):
        src, dst, recv, device = (
            (mine[kv].at[parts[0]], window.at[kv, 4, parts[0]], arrived.at[kv, 4, 0], at_chunk(4)),
            (mine[kv].at[parts[1]], transit.at[kv], passing.at[kv], at_chunk(-4)),
            (window.at[kv, 4, parts[0]], window.at[kv, 8, parts[0]], arrived.at[kv, 8, 0], at_chunk(4)),
            (transit.at[kv], window.at[kv, 8, parts[1]], arrived.at[kv, 8, 1], at_chunk(12)),
            (window.at[kv, 8, parts[1]], window.at[kv, 4, parts[1]], arrived.at[kv, 4, 1], at_chunk(-4)),
        )[step]
        return pltpu.make_async_remote_copy(
            src_ref=src,
            dst_ref=dst,
            send_sem=z_send.at[kv, step],
            recv_sem=recv,
            device_id=device,
            device_id_type=MESH,
        )

    def y_copy(kv, part, turn, message, src):
        slot = turn + 4 * message
        return pltpu.make_async_remote_copy(
            src_ref=src,
            dst_ref=window.at[kv, slot, parts[part]],
            send_sem=y_send.at[kv, turn - 1, message, part],
            recv_sem=arrived.at[kv, slot, part],
            device_id=at_y(turn),
            device_id_type=MESH,
        )

    def share(kv, part, slot):
        for turn in (1, 2, 3):
            ahead = lane_y + turn < 4
            src = mine[kv].at[parts[part]] if slot == 0 else window.at[kv, slot, parts[part]]
            if slot == 0 or slot == 4:
                @pl.when(ahead)
                def _():
                    y_copy(kv, part, turn, slot // 4, src).start()
            if slot == 4 or slot == 8:
                @pl.when(jnp.logical_not(ahead))
                def _():
                    y_copy(kv, part, turn, slot // 4 - 1, src).start()

    def wait_arrival(kv, slot, part):
        ref = window.at[kv, slot, parts[part]]
        pltpu.make_async_copy(ref, ref, arrived.at[kv, slot, part]).wait()

    def wait_passing(kv):
        pltpu.make_async_copy(transit.at[kv], transit.at[kv], passing.at[kv]).wait()

    for kv in (0, 1):
        z_copy(kv, 0).start()
        z_copy(kv, 1).start()
    for kv in (0, 1):
        for part in (0, 1):
            share(kv, part, 0)

    lengths = len_ref[...]
    count = lengths.shape[1]
    down = lax.broadcasted_iota(jnp.int32, (count, count), 0)
    across = lax.broadcasted_iota(jnp.int32, (count, count), 1)
    column = jnp.sum(jnp.where(down == across, lengths, 0), axis=1, keepdims=True)
    begins = jnp.sum(jnp.where(down < across, column, 0), axis=0, keepdims=True)
    base = chunk * ROWS
    positions = base + lax.broadcasted_iota(jnp.int32, (ROWS, 1), 0)
    starts = jnp.max(jnp.where(begins <= positions, begins, 0), axis=1, keepdims=True)
    key_lane = base + lax.broadcasted_iota(jnp.int32, (ROWS, ROWS), 1)
    for slot in range(SLOTS):
        keys_at = key_lane - slot * ROWS
        allowed = keys_at >= starts
        if slot == 0:
            allowed = allowed & (keys_at <= positions)
        bias[slot] = jnp.where(allowed, 0.0, MASKED)

    for copy in own:
        copy.wait()

    def score(first, slots, fresh):
        @pl.loop(0, KVH)
        def _(head):
            column = pl.multiple_of(head * HD, HD)
            stacked = jnp.concatenate(
                [q_own[:, pl.ds(pl.multiple_of(head * GROUP * HD + j * HD, HD), HD)] for j in range(GROUP)],
                axis=0,
            )
            peak = None if fresh else peaks[head]
            keys = window[0, pl.ds(first, slots), :, pl.ds(column, HD)].reshape(slots * ROWS, HD)
            raw = lax.dot_general(
                stacked, keys, (((1,), (1,)), ((), ())), preferred_element_type=jnp.float32
            ).reshape(GROUP, ROWS, slots * ROWS)
            for i in range(slots):
                masked = raw[:, :, i * ROWS : (i + 1) * ROWS] + bias[first + i][None]
                scores[first + i, head] = masked
                peak = masked if peak is None else jnp.maximum(peak, masked)
            peaks[head] = peak

    score(0, 1, True)

    for kv in (0, 1):
        wait_arrival(kv, 4, 0)
        z_copy(kv, 2).start()
        share(kv, 0, 4)
        wait_passing(kv)
        z_copy(kv, 3).start()
    for kv in (0, 1):
        wait_arrival(kv, 8, 1)
        z_copy(kv, 4).start()
        share(kv, 1, 8)
    for kv in (0, 1):
        wait_arrival(kv, 8, 0)
        share(kv, 0, 8)
        wait_arrival(kv, 4, 1)
        share(kv, 1, 4)

    for slot in (1, 2, 3, 5, 6, 7):
        for part in (0, 1):
            wait_arrival(0, slot, part)
    for first in (1, 3, 5, 7):
        score(first, 2, False)

    @pl.loop(0, QH)
    def _(index):
        head, j = index // GROUP, index % GROUP
        peak = jnp.max(peaks[head, j], axis=1, keepdims=True)
        total_weight = jnp.zeros((ROWS, ROWS), jnp.float32)
        for slot in range(SLOTS):
            weight = jnp.exp2((scores[slot, head, j] - peak) * SCALE)
            total_weight = total_weight + weight
            weights[head, j, :, slot * ROWS : (slot + 1) * ROWS] = weight.astype(jnp.bfloat16)
        row_sum = jnp.sum(total_weight, axis=1, keepdims=True)
        inverse[index] = jnp.broadcast_to(1.0 / row_sum, (ROWS, HD))

    for slot in (1, 2, 3, 5, 6, 7):
        for part in (0, 1):
            wait_arrival(1, slot, part)

    @pl.loop(0, KVH)
    def _(head):
        column = pl.multiple_of(head * HD, HD)
        values = window[1, :, :, pl.ds(column, HD)].reshape(SLOTS * ROWS, HD)
        mixed = jnp.dot(
            weights[head].reshape(GROUP * ROWS, SLOTS * ROWS), values, preferred_element_type=jnp.float32
        )
        for j in range(GROUP):
            place = pl.multiple_of(head * GROUP * HD + j * HD, HD)
            o_ref[:, pl.ds(place, HD)] = (
                mixed[j * ROWS : (j + 1) * ROWS] * inverse[head * GROUP + j]
            ).astype(jnp.bfloat16)

    for kv in (0, 1):
        for step in range(5):
            z_copy(kv, step).wait_send()
        for turn in (1, 2, 3):
            for message in (0, 1):
                for part in (0, 1):
                    y_copy(kv, part, turn, message, window.at[kv, 4, parts[part]]).wait_send()


def body(queries, key_proj, value_proj, seq_lengths):
    seq_size = lax.axis_size("seq")
    total = lax.axis_size("dp") * seq_size
    rows_behind = ROWS - AHEAD
    return pl.pallas_call(
        functools.partial(kernel, seq_size, total),
        out_shape=jax.ShapeDtypeStruct((ROWS, QH * HD), jnp.bfloat16),
        in_specs=[
            pl.BlockSpec(memory_space=pltpu.VMEM),
            pl.BlockSpec(memory_space=pl.ANY),
            pl.BlockSpec(memory_space=pl.ANY),
            pl.BlockSpec(memory_space=pl.ANY),
        ],
        out_specs=pl.BlockSpec(memory_space=pltpu.VMEM),
        scratch_shapes=[
            pltpu.VMEM((ROWS, QH * HD), jnp.bfloat16),
            pltpu.VMEM((2, SLOTS, ROWS, KVH * HD), jnp.bfloat16),
            pltpu.VMEM((2, rows_behind, KVH * HD), jnp.bfloat16),
            pltpu.VMEM((SLOTS, KVH, GROUP, ROWS, ROWS), jnp.float32),
            pltpu.VMEM((KVH, GROUP, ROWS, SLOTS * ROWS), jnp.bfloat16),
            pltpu.VMEM((KVH, GROUP, ROWS, ROWS), jnp.float32),
            pltpu.VMEM((QH, ROWS, HD), jnp.float32),
            pltpu.VMEM((SLOTS, ROWS, ROWS), jnp.float32),
            pltpu.SemaphoreType.DMA((3,)),
            pltpu.SemaphoreType.DMA((2, 5)),
            pltpu.SemaphoreType.DMA((2, 3, 2, 2)),
            pltpu.SemaphoreType.DMA((2, SLOTS, 2)),
            pltpu.SemaphoreType.DMA((2,)),
        ],
        compiler_params=pltpu.CompilerParams(
            collective_id=0, has_side_effects=True, vmem_limit_bytes=52 * 2**20
        ),
    )(seq_lengths.reshape(1, -1), queries, key_proj, value_proj)


def solution(mesh):
    return jax.shard_map(
        body,
        mesh=mesh,
        in_specs=(P(("dp", "seq"), None), P(("dp", "seq"), None), P(("dp", "seq"), None), P()),
        out_specs=P(("dp", "seq"), None),
        check_vma=False,
    )
```

time: 410 us -> 118 us (0.29)
  the two profiles are of different devices: /device:TPU:70 before, /device:TPU:99 now
where the time goes in v1:
time: 118 us
  Pallas kernels  114 us (97%)
  local copies, waits for them, and re-layouts  3.46 us (3%)
    pallas_call x1, Pallas kernels, body(): pl.pallas_call(functools.partial(kernel, seq_size, total), out_shape=jax....  114 us
    unnamed x7, local copies, waits for them, and re-layouts  3.46 us

profile of v1, /device:TPU:99, one launch (start us, length us, event | category | flops | bytes accessed | tf_op | source)
XLA Modules:
  0.0 117.8 jit_solution(3721381431586168614)
XLA Ops:
  0.0 0.0 copy-start.2
  0.0 0.7 copy-done.2
  0.7 0.0 copy-start
  0.7 0.9 copy-done
  1.6 0.0 copy-start.1
  1.6 0.9 copy-done.1
  2.5 114.3 %shard_map.46 = bf16[128,4096]{1,0:T(8,128)(2,1)S(1)} custom-call(s32[1,256]{1,0:T(1,128)S(1)} %bitcast.1, bf16[128,4096]{1,0:T(8,128)(2,1)} %q_ref.1, bf16[128,512]{1,0:T(8,128)(2,1)S(1)} %copy-done, bf16[128,512]{1,0:T(8,128)(2,1)S(1)} %copy-done.1), custom_call_target="tpu_custom_call" | custom-call | tf_op jit(solution)/shard_map/pallas_call | solution.py:232
  116.8 1.0 copy.6
Async XLA Ops:
  0.0 0.7 copy-start.2
  0.7 0.9 copy-start
  1.6 0.9 copy-start.1

commit v2 on v1

v2 whole, which is shorter than its diff:
```python
import functools

import jax
import jax.numpy as jnp
from jax import lax
from jax.experimental import pallas as pl
from jax.experimental.pallas import tpu as pltpu
from jax.sharding import PartitionSpec as P

HD = 128
QH = 32
KVH = 4
GROUP = QH // KVH
ROWS = 128
SLOTS = 9
FORWARD = ((0, 48), (48, 32))
BACKWARD = ((80, 32), (112, 16))
BACK_FIRST = BACKWARD[0][0]
SCALE = 0.08838834764831845 * 1.4426950408889634
MASKED = -1e30
MESH = pl.DeviceIdType.MESH


AHEAD_TIMES = ((0.25, 0.55), (0.75, 1.0))
BACK_TIMES = ((0.17, 0.37, 0.57), (0.67, 0.83, 1.0))


def schedule():
    events = []
    for what, pieces, times in (("ahead", FORWARD, AHEAD_TIMES), ("back", BACKWARD, BACK_TIMES)):
        for kv in (0, 1):
            for hop, time in enumerate(times[kv]):
                for i in range(len(pieces)):
                    events.append((time - 0.12 * (1 - (i + 1) / len(pieces)), what, kv, hop, i))
    return [event[1:] for event in sorted(events)]


def kernel(
    seq_size,
    total,
    len_ref,
    q_ref,
    k_ref,
    v_ref,
    o_ref,
    q_own,
    window,
    transit,
    scores,
    weights,
    peaks,
    inverse,
    bias,
    local_sem,
    z_send,
    y_send,
    ahead_sem,
    back_sem,
    y_sem,
):
    dp = lax.axis_index("dp")
    seq = lax.axis_index("seq")
    chunk = dp * seq_size + seq
    lane_y = seq % 4

    def at_chunk(offset):
        other = (chunk + offset + total) % total
        return (other // seq_size, other % seq_size)

    def at_y(turn):
        return (dp, seq - lane_y + (lane_y + turn) % 4)

    own = [
        pltpu.make_async_copy(q_ref, q_own, local_sem.at[0]),
        pltpu.make_async_copy(k_ref, window.at[0, 0], local_sem.at[1]),
        pltpu.make_async_copy(v_ref, window.at[1, 0], local_sem.at[2]),
    ]
    for copy in own:
        copy.start()

    barrier = pltpu.get_barrier_semaphore()
    for device in (at_chunk(-4), at_chunk(4), at_chunk(-12), at_y(1), at_y(2), at_y(3)):
        pl.semaphore_signal(barrier, inc=1, device_id=device, device_id_type=MESH)

    mine = (k_ref, v_ref)

    def passing_rows(piece):
        first, count = piece
        return pl.ds(first - BACK_FIRST, count)

    def send_ahead(kv, hop, i):
        rows = pl.ds(*FORWARD[i])
        pltpu.make_async_remote_copy(
            src_ref=mine[kv].at[rows] if hop == 0 else window.at[kv, 4, rows],
            dst_ref=window.at[kv, 4 + 4 * hop, rows],
            send_sem=z_send.at[kv, hop],
            recv_sem=ahead_sem.at[kv, hop, i],
            device_id=at_chunk(4),
            device_id_type=MESH,
        ).start()

    def send_back(kv, hop, i):
        rows = pl.ds(*BACKWARD[i])
        passed = transit.at[kv, passing_rows(BACKWARD[i])]
        pltpu.make_async_remote_copy(
            src_ref=(mine[kv].at[rows], passed, window.at[kv, 8, rows])[hop],
            dst_ref=(passed, window.at[kv, 8, rows], window.at[kv, 4, rows])[hop],
            send_sem=z_send.at[kv, hop],
            recv_sem=back_sem.at[kv, hop, i],
            device_id=at_chunk((-4, 12, -4)[hop]),
            device_id_type=MESH,
        ).start()

    def y_copy(kv, turn, message, src, rows):
        slot = turn + 4 * message
        return pltpu.make_async_remote_copy(
            src_ref=src,
            dst_ref=window.at[kv, slot, rows],
            send_sem=y_send.at[kv, turn - 1, message],
            recv_sem=y_sem.at[kv, slot],
            device_id=at_y(turn),
            device_id_type=MESH,
        )

    def share(kv, slot, rows):
        src = mine[kv].at[rows] if slot == 0 else window.at[kv, slot, rows]
        for turn in (1, 2, 3):
            ahead = lane_y + turn < 4
            if slot < 8:

                @pl.when(ahead)
                def _():
                    y_copy(kv, turn, slot // 4, src, rows).start()

            if slot > 0:

                @pl.when(jnp.logical_not(ahead))
                def _():
                    y_copy(kv, turn, slot // 4 - 1, src, rows).start()

    def arrive(what, kv, hop, i):
        rows = pl.ds(*(FORWARD if what == "ahead" else BACKWARD)[i])
        if what == "ahead":
            ref = window.at[kv, 4 + 4 * hop, rows]
            pltpu.make_async_copy(ref, ref, ahead_sem.at[kv, hop, i]).wait()
            if hop == 0:
                send_ahead(kv, 1, i)
                if kv == 0:
                    send_ahead(1, 0, i)
            share(kv, 4 + 4 * hop, rows)
        else:
            ref = (
                transit.at[kv, passing_rows(BACKWARD[i])],
                window.at[kv, 8, rows],
                window.at[kv, 4, rows],
            )[hop]
            pltpu.make_async_copy(ref, ref, back_sem.at[kv, hop, i]).wait()
            if hop < 2:
                send_back(kv, hop + 1, i)
                if kv == 0 and hop == 0:
                    send_back(1, 0, i)
            if hop > 0:
                share(kv, 12 - 4 * hop, rows)

    def await_slot(kv, slot):
        ref = window.at[kv, slot]
        pltpu.make_async_copy(ref, ref, y_sem.at[kv, slot]).wait()

    lengths = len_ref[...]
    count = lengths.shape[1]
    down = lax.broadcasted_iota(jnp.int32, (count, count), 0)
    across = lax.broadcasted_iota(jnp.int32, (count, count), 1)
    column = jnp.sum(jnp.where(down == across, lengths, 0), axis=1, keepdims=True)
    begins = jnp.sum(jnp.where(down < across, column, 0), axis=0, keepdims=True)
    base = chunk * ROWS
    positions = base + lax.broadcasted_iota(jnp.int32, (ROWS, 1), 0)
    starts = jnp.max(jnp.where(begins <= positions, begins, 0), axis=1, keepdims=True)
    key_lane = base + lax.broadcasted_iota(jnp.int32, (ROWS, ROWS), 1)
    for slot in range(SLOTS):
        keys_at = key_lane - slot * ROWS
        allowed = keys_at >= starts
        if slot == 0:
            allowed = allowed & (keys_at <= positions)
        bias[slot] = jnp.where(allowed, 0.0, MASKED)

    pl.semaphore_wait(barrier, 6)
    for i in range(len(FORWARD)):
        send_ahead(0, 0, i)
    for i in range(len(BACKWARD)):
        send_back(0, 0, i)
    for kv in (0, 1):
        share(kv, 0, pl.ds(0, ROWS))

    for copy in own:
        copy.wait()

    def score(first, slots):
        @pl.loop(0, KVH)
        def _(head):
            column = pl.multiple_of(head * HD, HD)
            stacked = jnp.concatenate(
                [q_own[:, pl.ds(pl.multiple_of(head * GROUP * HD + j * HD, HD), HD)] for j in range(GROUP)],
                axis=0,
            )
            peak = None if first == 0 else peaks[head]
            keys = window[0, pl.ds(first, slots), :, pl.ds(column, HD)].reshape(slots * ROWS, HD)
            raw = lax.dot_general(
                stacked, keys, (((1,), (1,)), ((), ())), preferred_element_type=jnp.float32
            ).reshape(GROUP, ROWS, slots * ROWS)
            for i in range(slots):
                masked = raw[:, :, i * ROWS : (i + 1) * ROWS] + bias[first + i][None]
                scores[first + i, head] = masked
                peak = masked if peak is None else jnp.maximum(peak, masked)
            peaks[head] = peak

    def weigh(head):
        @pl.loop(0, GROUP)
        def _(j):
            peak = jnp.max(peaks[head, j], axis=1, keepdims=True)
            total_weight = jnp.zeros((ROWS, ROWS), jnp.float32)
            for slot in range(SLOTS):
                weight = jnp.exp2((scores[slot, head, j] - peak) * SCALE)
                total_weight = total_weight + weight
                weights[head, j, :, slot * ROWS : (slot + 1) * ROWS] = weight.astype(jnp.bfloat16)
            row_sum = jnp.sum(total_weight, axis=1, keepdims=True)
            inverse[head * GROUP + j] = jnp.broadcast_to(1.0 / row_sum, (ROWS, HD))

    score(0, 1)

    def mix(head, slots):
        values = jnp.concatenate([window[1, slot, :, pl.ds(pl.multiple_of(head * HD, HD), HD)] for slot in slots], axis=0)
        shares = jnp.concatenate([weights[head, :, :, slot * ROWS : (slot + 1) * ROWS] for slot in slots], axis=2)
        return jnp.dot(
            shares.reshape(GROUP * ROWS, len(slots) * ROWS), values, preferred_element_type=jnp.float32
        ).reshape(GROUP, ROWS, HD)

    events = schedule()
    keys_last = max(i for i, event in enumerate(events) if event[1] == 0)
    work = [functools.partial(score, first, 2) for first in (1, 3, 5, 7)]
    work += [functools.partial(weigh, head) for head in range(KVH)]
    last = [i for i in range(keys_last, len(events)) if events[i][2] < 2 - (events[i][0] == "ahead")]
    for i, event in enumerate(events):
        arrive(*event)
        if i == keys_last:
            for slot in (1, 2, 3, 5, 6, 7):
                await_slot(0, slot)
        if i in last:
            done = 8 * (last.index(i) + 1) // len(last) - 8 * last.index(i) // len(last)
            for _ in range(done):
                work.pop(0)()
    for step in work:
        step()

    along_y = (1, 2, 3, 5, 6, 7)

    @pl.loop(0, KVH)
    def _(head):
        peaks[head] = mix(head, (0, 4, 8))

    for slot in along_y:
        await_slot(1, slot)

    @pl.loop(0, KVH)
    def _(head):
        mixed = peaks[head] + mix(head, along_y)
        for j in range(GROUP):
            place = pl.multiple_of(head * GROUP * HD + j * HD, HD)
            o_ref[:, pl.ds(place, HD)] = (mixed[j] * inverse[head * GROUP + j]).astype(jnp.bfloat16)

    for kv in (0, 1):
        whole = window.at[kv, 0]
        for hop in (0, 1):
            pltpu.make_async_copy(whole, whole, z_send.at[kv, hop]).wait()
        pltpu.make_async_copy(transit.at[kv], transit.at[kv], z_send.at[kv, 2]).wait()
        for turn in (1, 2, 3):
            for message in (0, 1):
                pltpu.make_async_copy(whole, whole, y_send.at[kv, turn - 1, message]).wait()


def body(queries, key_proj, value_proj, seq_lengths):
    seq_size = lax.axis_size("seq")
    total = lax.axis_size("dp") * seq_size
    return pl.pallas_call(
        functools.partial(kernel, seq_size, total),
        out_shape=jax.ShapeDtypeStruct((ROWS, QH * HD), jnp.bfloat16),
        in_specs=[
            pl.BlockSpec(memory_space=pltpu.VMEM),
            pl.BlockSpec(memory_space=pl.ANY),
            pl.BlockSpec(memory_space=pl.ANY),
            pl.BlockSpec(memory_space=pl.ANY),
        ],
        out_specs=pl.BlockSpec(memory_space=pltpu.VMEM),
        scratch_shapes=[
            pltpu.VMEM((ROWS, QH * HD), jnp.bfloat16),
            pltpu.VMEM((2, SLOTS, ROWS, KVH * HD), jnp.bfloat16),
            pltpu.VMEM((2, ROWS - BACK_FIRST, KVH * HD), jnp.bfloat16),
            pltpu.VMEM((SLOTS, KVH, GROUP, ROWS, ROWS), jnp.float32),
            pltpu.VMEM((KVH, GROUP, ROWS, SLOTS * ROWS), jnp.bfloat16),
            pltpu.VMEM((KVH, GROUP, ROWS, ROWS), jnp.float32),
            pltpu.VMEM((QH, ROWS, HD), jnp.float32),
            pltpu.VMEM((SLOTS, ROWS, ROWS), jnp.float32),
            pltpu.SemaphoreType.DMA((3,)),
            pltpu.SemaphoreType.DMA((2, 3)),
            pltpu.SemaphoreType.DMA((2, 3, 2)),
            pltpu.SemaphoreType.DMA((2, 2, len(FORWARD))),
            pltpu.SemaphoreType.DMA((2, 3, len(BACKWARD))),
            pltpu.SemaphoreType.DMA((2, SLOTS)),
        ],
        compiler_params=pltpu.CompilerParams(
            collective_id=0, has_side_effects=True, vmem_limit_bytes=60 * 2**20
        ),
    )(seq_lengths.reshape(1, -1), queries, key_proj, value_proj)


def solution(mesh):
    return jax.shard_map(
        body,
        mesh=mesh,
        in_specs=(P(("dp", "seq"), None), P(("dp", "seq"), None), P(("dp", "seq"), None), P()),
        out_specs=P(("dp", "seq"), None),
        check_vma=False,
    )
```

time: 118 us -> 108 us (0.915)
  the two profiles are of different devices: /device:TPU:99 before, /device:TPU:1 now
where the time goes in v2:
time: 108 us; the launch traced here: 107 us
  Pallas kernels  105 us (97%)
  local copies, waits for them, and re-layouts  2.29 us (2%)
    pallas_call x1, Pallas kernels, body(): pl.pallas_call(functools.partial(kernel, seq_size, total), out_shape=jax....  105 us
    unnamed x1, local copies, waits for them, and re-layouts  2.29 us

profile of v2, /device:TPU:1, one launch (start us, length us, event | category | flops | bytes accessed | tf_op | source)
XLA Modules:
  0.0 107.4 jit_solution(3552536936823579855)
XLA Ops:
  0.0 105.1 %shard_map.46 = bf16[128,4096]{1,0:T(8,128)(2,1)} custom-call(s32[1,256]{1,0:T(1,128)} %bitcast.1, bf16[128,4096]{1,0:T(8,128)(2,1)} %q_ref.1, bf16[128,512]{1,0:T(8,128)(2,1)} %k_ref.1, bf16[128,512]{1,0:T(8,128)(2,1)} %v_ref.1), custom_call_target="tpu_custom_call" | custom-call | tf_op jit(solution)/shard_map/pallas_call | solution.py:283
  105.1 2.3 %copy.6 = bf16[128,4096]{1,0:T(8,128)(2,1)} copy(bf16[128,4096]{1,0:T(8,128)(2,1)} %shard_map.46) | data formatting | bytes 2097152

commit v3 on v2

--- a/solution.py
+++ b/solution.py
@@ -22,7 +22,7 @@
 
 
 AHEAD_TIMES = ((0.25, 0.55), (0.75, 1.0))
-BACK_TIMES = ((0.17, 0.37, 0.57), (0.67, 0.83, 1.0))
+BACK_TIMES = ((0.17, 0.4, 0.6), (0.5, 0.8, 1.0))
 
 
 def schedule():
@@ -157,8 +157,6 @@
             pltpu.make_async_copy(ref, ref, back_sem.at[kv, hop, i]).wait()
             if hop < 2:
                 send_back(kv, hop + 1, i)
-                if kv == 0 and hop == 0:
-                    send_back(1, 0, i)
             if hop > 0:
                 share(kv, 12 - 4 * hop, rows)
 
@@ -186,8 +184,9 @@
     pl.semaphore_wait(barrier, 6)
     for i in range(len(FORWARD)):
         send_ahead(0, 0, i)
-    for i in range(len(BACKWARD)):
-        send_back(0, 0, i)
+    for kv in (0, 1):
+        for i in range(len(BACKWARD)):
+            send_back(kv, 0, i)
     for kv in (0, 1):
         share(kv, 0, pl.ds(0, ROWS))
 

time: 108 us -> 103 us (0.954)
  the two profiles are of different devices: /device:TPU:1 before, /device:TPU:16 now
where the time goes in v3:
time: 103 us
  Pallas kernels  101 us (98%)
  local copies, waits for them, and re-layouts  2.29 us (2%)
    pallas_call x1, Pallas kernels, body(): pl.pallas_call(functools.partial(kernel, seq_size, total), out_shape=jax....  101 us
    unnamed x1, local copies, waits for them, and re-layouts  2.29 us

profile of v3, /device:TPU:16, one launch (start us, length us, event | category | flops | bytes accessed | tf_op | source)
XLA Modules:
  0.0 103.3 jit_solution(9964595614332904650)
XLA Ops:
  0.0 101.0 %shard_map.46 = bf16[128,4096]{1,0:T(8,128)(2,1)} custom-call(s32[1,256]{1,0:T(1,128)} %bitcast.1, bf16[128,4096]{1,0:T(8,128)(2,1)} %q_ref.1, bf16[128,512]{1,0:T(8,128)(2,1)} %k_ref.1, bf16[128,512]{1,0:T(8,128)(2,1)} %v_ref.1), custom_call_target="tpu_custom_call" | custom-call | tf_op jit(solution)/shard_map/pallas_call | solution.py:282
  101.0 2.3 %copy.6 = bf16[128,4096]{1,0:T(8,128)(2,1)} copy(bf16[128,4096]{1,0:T(8,128)(2,1)} %shard_map.46) | data formatting | bytes 2097152

commit v4 on v3

--- a/solution.py
+++ b/solution.py
@@ -43,6 +43,7 @@
     k_ref,
     v_ref,
     o_ref,
+    lengths_own,
     q_own,
     window,
     transit,
@@ -71,6 +72,7 @@
         return (dp, seq - lane_y + (lane_y + turn) % 4)
 
     own = [
+        pltpu.make_async_copy(len_ref, lengths_own, local_sem.at[3]),
         pltpu.make_async_copy(q_ref, q_own, local_sem.at[0]),
         pltpu.make_async_copy(k_ref, window.at[0, 0], local_sem.at[1]),
         pltpu.make_async_copy(v_ref, window.at[1, 0], local_sem.at[2]),
@@ -164,7 +166,8 @@
         ref = window.at[kv, slot]
         pltpu.make_async_copy(ref, ref, y_sem.at[kv, slot]).wait()
 
-    lengths = len_ref[...]
+    own[0].wait()
+    lengths = lengths_own[...]
     count = lengths.shape[1]
     down = lax.broadcasted_iota(jnp.int32, (count, count), 0)
     across = lax.broadcasted_iota(jnp.int32, (count, count), 1)
@@ -190,7 +193,7 @@
     for kv in (0, 1):
         share(kv, 0, pl.ds(0, ROWS))
 
-    for copy in own:
+    for copy in own[1:]:
         copy.wait()
 
     def score(first, slots):
@@ -207,7 +210,7 @@
                 stacked, keys, (((1,), (1,)), ((), ())), preferred_element_type=jnp.float32
             ).reshape(GROUP, ROWS, slots * ROWS)
             for i in range(slots):
-                masked = raw[:, :, i * ROWS : (i + 1) * ROWS] + bias[first + i][None]
+                masked = raw[:, :, i * ROWS : (i + 1) * ROWS] * SCALE + bias[first + i][None]
                 scores[first + i, head] = masked
                 peak = masked if peak is None else jnp.maximum(peak, masked)
             peaks[head] = peak
@@ -218,7 +221,7 @@
             peak = jnp.max(peaks[head, j], axis=1, keepdims=True)
             total_weight = jnp.zeros((ROWS, ROWS), jnp.float32)
             for slot in range(SLOTS):
-                weight = jnp.exp2((scores[slot, head, j] - peak) * SCALE)
+                weight = jnp.exp2(scores[slot, head, j] - peak)
                 total_weight = total_weight + weight
                 weights[head, j, :, slot * ROWS : (slot + 1) * ROWS] = weight.astype(jnp.bfloat16)
             row_sum = jnp.sum(total_weight, axis=1, keepdims=True)
@@ -283,13 +286,14 @@
         functools.partial(kernel, seq_size, total),
         out_shape=jax.ShapeDtypeStruct((ROWS, QH * HD), jnp.bfloat16),
         in_specs=[
-            pl.BlockSpec(memory_space=pltpu.VMEM),
-            pl.BlockSpec(memory_space=pl.ANY),
-            pl.BlockSpec(memory_space=pl.ANY),
-            pl.BlockSpec(memory_space=pl.ANY),
+            pl.BlockSpec(memory_space=pltpu.HBM),
+            pl.BlockSpec(memory_space=pltpu.HBM),
+            pl.BlockSpec(memory_space=pltpu.HBM),
+            pl.BlockSpec(memory_space=pltpu.HBM),
         ],
         out_specs=pl.BlockSpec(memory_space=pltpu.VMEM),
         scratch_shapes=[
+            pltpu.VMEM((1, seq_lengths.shape[0]), jnp.int32),
             pltpu.VMEM((ROWS, QH * HD), jnp.bfloat16),
             pltpu.VMEM((2, SLOTS, ROWS, KVH * HD), jnp.bfloat16),
             pltpu.VMEM((2, ROWS - BACK_FIRST, KVH * HD), jnp.bfloat16),
@@ -298,7 +302,7 @@
             pltpu.VMEM((KVH, GROUP, ROWS, ROWS), jnp.float32),
             pltpu.VMEM((QH, ROWS, HD), jnp.float32),
             pltpu.VMEM((SLOTS, ROWS, ROWS), jnp.float32),
-            pltpu.SemaphoreType.DMA((3,)),
+            pltpu.SemaphoreType.DMA((4,)),
             pltpu.SemaphoreType.DMA((2, 3)),
             pltpu.SemaphoreType.DMA((2, 3, 2)),
             pltpu.SemaphoreType.DMA((2, 2, len(FORWARD))),

time: 103 us -> 104 us (level)
  the two profiles are of different devices: /device:TPU:16 before, /device:TPU:96 now
where the time goes in v4:
time: 104 us
  Pallas kernels  101 us (97%)
  local copies, waits for them, and re-layouts  2.29 us (2%)
    pallas_call x1, Pallas kernels, body(): pl.pallas_call(functools.partial(kernel, seq_size, total), out_shape=jax....  101 us
    unnamed x1, local copies, waits for them, and re-layouts  2.29 us

profile of v4, /device:TPU:96, one launch (start us, length us, event | category | flops | bytes accessed | tf_op | source)
XLA Modules:
  0.0 103.6 jit_solution(14812147756819841645)
XLA Ops:
  0.0 101.3 %shard_map.46 = bf16[128,4096]{1,0:T(8,128)(2,1)} custom-call(s32[1,256]{1,0:T(1,128)} %bitcast.1, bf16[128,4096]{1,0:T(8,128)(2,1)} %q_ref.1, bf16[128,512]{1,0:T(8,128)(2,1)} %k_ref.1, bf16[128,512]{1,0:T(8,128)(2,1)} %v_ref.1), custom_call_target="tpu_custom_call" | custom-call | tf_op jit(solution)/shard_map/pallas_call | solution.py:285
  101.3 2.3 %copy.6 = bf16[128,4096]{1,0:T(8,128)(2,1)} copy(bf16[128,4096]{1,0:T(8,128)(2,1)} %shard_map.46) | data formatting | bytes 2097152
